TPU v7x, 32 devices: a whole 2x2x4 slice. The times are simulated.
32 devices in a mesh: groups: 2 (over y), batch: 4 (over z), tensor: 4 (over x, core).
Axes of the slice: x: 2, y: 2, z: 4, core: 2. Of those that a mesh axis runs over, the one named last changes fastest.
Arguments:
- hidden: bfloat16 [8, 8192], P(('groups', 'batch')), parts along dimension 0, may hold values from -6 to 6
- self_norm: bfloat16 [8192], replicated, may hold values from 0.5 to 1.5
- self_query: bfloat16 [8192, 8192], P('batch', 'tensor'), may hold values from -0.0625 to 0.0625
- self_keyval: bfloat16 [8192, 2048], P('batch', 'tensor'), may hold values from -0.0625 to 0.0625
- self_output: bfloat16 [8192, 8192], P('tensor', 'batch'), may hold values from -0.0625 to 0.0625
- key_cache: bfloat16 [8, 1024, 2048], P(('groups', 'batch'), None, 'tensor'), parts along dimension 0, may hold values from -6 to 6
- cache_lengths: int32 [8], P(('groups', 'batch')), parts along dimension 0, may hold values from 1 to 1024, as said below
- cross_norm: bfloat16 [8192], replicated, may hold values from 0.5 to 1.5
- cross_query: bfloat16 [8192, 8192], P('batch', 'tensor'), may hold values from -0.0625 to 0.0625
- query_gain: float32 [128], replicated, may hold values from 0.5 to 2
- key_gain: float32 [128], replicated, may hold values from 0.5 to 2
- cross_output: bfloat16 [8192, 8192], P('tensor', 'batch'), may hold values from -0.0625 to 0.0625
- cross_gate: float32 [1], replicated, may hold values from 0.3 to 1.2
- image_keyval: bfloat16 [32, 320, 2048], P(('groups', 'batch'), None, 'tensor'), parts along dimension 0, may hold values from -6 to 6
- tile_count: int32 [8], P('groups'), parts along dimension 0, may hold values from 1 to 4
- tile_place: int32 [8, 4], P('groups'), parts along dimension 0, may hold values from 0 to 15, as said below
Outputs:
- layer_output: bfloat16 [8, 8192], P(('groups', 'batch')), parts along dimension 0
There are 2 independent parts, one for each index of `groups`. A program takes and returns all parts, laid end to end along the dimension named above; an argument that names none is the same for every part. Nothing has to cross between parts.
Inputs may be any that keep to these rules, and one draw needn't show every extreme that they name: The new token takes position cache_lengths; cache positions at or above it are unused. `tile_place`: all 16 entries differ; entries for tiles at or above tile_count name rows that no request uses.
All inputs are finite; a program needn't handle non-finite values.
Results may differ from a plain program's by a relative error of at most 0.009.
Values may be sent and summed in bfloat16 or wider, within the bound.
A program may use at most 128 MiB of HBM per device.

v0:
```python
import jax
import jax.numpy as jnp
from jax import lax
from jax.sharding import PartitionSpec as P

HEAD_DIM = 128
MAX_TILES = 4


EPSILON = 1e-05
THETA = 500000.0


def normalize(values, gains):
    values = values.astype(jnp.float32)
    factor = lax.rsqrt(jnp.mean(values * values, axis=-1, keepdims=True) + EPSILON)
    return values * factor * gains.astype(jnp.float32)


def rotate(values, positions):
    half_dim = values.shape[-1] // 2
    frequency = THETA ** (-(jnp.arange(half_dim, dtype=jnp.float32) * 2.0 / values.shape[-1]))
    angles = positions[:, None] * frequency[None, :]
    cosine = jnp.cos(angles)[:, None, :]
    sine_table = jnp.sin(angles)[:, None, :]
    lower_half = values[..., :half_dim]
    upper_half = values[..., half_dim:]
    return jnp.concatenate(
        [
            lower_half * cosine - upper_half * sine_table,
            upper_half * cosine + lower_half * sine_table,
        ],
        axis=-1,
    )


def back_project(values, weight):
    partial_rows = jnp.dot(
        lax.all_gather(values, "batch", axis=0, tiled=True),
        weight,
        preferred_element_type=jnp.float32,
    )
    summed = lax.psum(partial_rows, "tensor")
    return lax.all_to_all(summed, "batch", split_axis=0, concat_axis=1, tiled=True)


def per_device(
    hidden,
    self_norm,
    self_query,
    self_keyval,
    self_output,
    key_cache,
    cache_lengths,
    cross_norm,
    cross_query,
    query_gain,
    key_gain,
    cross_output,
    cross_gate,
    image_keyval,
    tile_count,
    tile_place,
):
    own_rows = hidden.shape[0]
    devices = lax.axis_size("batch")
    position = lax.axis_index("batch")
    requests = own_rows * devices
    local_heads = self_query.shape[1] // HEAD_DIM
    local_kv = self_keyval.shape[1] // (2 * HEAD_DIM)
    group_size = local_heads // local_kv
    head_width = local_heads * HEAD_DIM
    score_scale = HEAD_DIM ** (-0.5)
    cache_size = key_cache.shape[1]
    normed = normalize(hidden, self_norm).astype(jnp.bfloat16)
    columns = lax.all_to_all(normed, "batch", split_axis=1, concat_axis=0, tiled=True)
    picked = columns
    query_part = jnp.dot(picked, self_query, preferred_element_type=jnp.float32)
    keyval_part = jnp.dot(picked, self_keyval, preferred_element_type=jnp.float32)
    projected = lax.psum_scatter(
        jnp.concatenate([query_part, keyval_part], axis=1), "batch", scatter_dimension=0, tiled=True
    )
    positions = cache_lengths.astype(jnp.float32)
    queries = rotate(
        projected[:, :head_width].reshape(own_rows, local_heads, HEAD_DIM), positions
    ).astype(jnp.bfloat16)
    fresh_rows = projected[:, head_width:].reshape(own_rows, local_kv, 2, HEAD_DIM)
    fresh_key = rotate(fresh_rows[:, :, 0], positions).astype(jnp.bfloat16)
    fresh_value = fresh_rows[:, :, 1].astype(jnp.bfloat16)
    cache_rows = key_cache.reshape(own_rows, cache_size, local_kv, 2, HEAD_DIM)
    grouped = queries.reshape(own_rows, local_kv, group_size, HEAD_DIM)
    scores = (
        jnp.einsum(
            "rkgd,rtkd->rkgt", grouped, cache_rows[:, :, :, 0], preferred_element_type=jnp.float32
        )
        * score_scale
    )
    usable = jnp.arange(cache_size)[None, :] < cache_lengths[:, None]
    scores = jnp.where(usable[:, None, None, :], scores, -jnp.inf)
    own_score = (
        jnp.einsum("rkgd,rkd->rkg", grouped, fresh_key, preferred_element_type=jnp.float32)
        * score_scale
    )
    top_score = jnp.maximum(jnp.max(scores, axis=-1), own_score)
    weights = jnp.exp(scores - top_score[..., None])
    own_weight = jnp.exp(own_score - top_score)
    total_weight = jnp.sum(weights, axis=-1) + own_weight
    probabilities = (weights / total_weight[..., None]).astype(jnp.bfloat16)
    own_prob = (own_weight / total_weight).astype(jnp.bfloat16)
    mixed_heads = jnp.einsum(
        "rkgt,rtkd->rkgd", probabilities, cache_rows[:, :, :, 1], preferred_element_type=jnp.float32
    )
    mixed_heads = (
        mixed_heads
        + own_prob.astype(jnp.float32)[..., None] * fresh_value.astype(jnp.float32)[:, :, None, :]
    )
    attended = mixed_heads.reshape(own_rows, head_width).astype(jnp.bfloat16)
    residual = (hidden.astype(jnp.float32) + back_project(attended, self_output)).astype(
        jnp.bfloat16
    )
    normed_cross = normalize(residual, cross_norm).astype(jnp.bfloat16)
    cross_columns = lax.all_to_all(normed_cross, "batch", split_axis=1, concat_axis=0, tiled=True)
    picked = cross_columns
    cross_raw = lax.psum_scatter(
        jnp.dot(picked, cross_query, preferred_element_type=jnp.float32).astype(jnp.bfloat16),
        "batch",
        scatter_dimension=0,
        tiled=True,
    ).astype(jnp.float32)
    cross_queries = (
        normalize(cross_raw.reshape(own_rows, local_heads, HEAD_DIM), query_gain)
        .astype(jnp.bfloat16)
        .reshape(own_rows, head_width)
    )
    every_query = lax.all_gather(cross_queries, "batch", axis=0, tiled=True)
    slot_count = image_keyval.shape[0]
    places = position * slot_count + jnp.arange(slot_count, dtype=jnp.int32)
    matches = (tile_place.reshape(-1)[None, :] == places[:, None]).reshape(
        slot_count, requests, MAX_TILES
    )
    owner_mask = jnp.any(matches, axis=2)
    slot_query = jnp.dot(
        owner_mask.astype(jnp.bfloat16), every_query, preferred_element_type=jnp.float32
    ).astype(jnp.bfloat16)
    tile_rows = image_keyval.reshape(slot_count, image_keyval.shape[1], local_kv, 2, HEAD_DIM)
    image_keys = normalize(tile_rows[:, :, :, 0], key_gain).astype(jnp.bfloat16)
    image_values = tile_rows[:, :, :, 1]
    slot_grouped = slot_query.reshape(slot_count, local_kv, group_size, HEAD_DIM)
    tile_scores = (
        jnp.einsum("skgd,stkd->skgt", slot_grouped, image_keys, preferred_element_type=jnp.float32)
        * score_scale
    )
    tile_top = jnp.max(tile_scores, axis=-1)
    tile_exp = jnp.exp(tile_scores - tile_top[..., None])
    tile_sum = jnp.sum(tile_exp, axis=-1)
    tile_out = jnp.einsum(
        "skgt,stkd->skgd",
        tile_exp.astype(jnp.bfloat16),
        image_values,
        preferred_element_type=jnp.float32,
    )
    flat_out = tile_out.reshape(slot_count, head_width)
    flat_top = tile_top.reshape(slot_count, local_heads)
    flat_sum = tile_sum.reshape(slot_count, local_heads)
    all_out, all_top, all_sum = (
        lax.all_gather(flat_out, "batch", axis=0, tiled=True),
        lax.all_gather(flat_top, "batch", axis=0, tiled=True),
        lax.all_gather(flat_sum, "batch", axis=0, tiled=True),
    )
    own_places = lax.dynamic_slice_in_dim(tile_place, position * own_rows, own_rows, 0).reshape(-1)
    own_counts = lax.dynamic_slice_in_dim(tile_count, position * own_rows, own_rows, 0)
    live_tile = jnp.arange(MAX_TILES)[None, :] < own_counts[:, None]
    picked_out = jnp.take(all_out, own_places, axis=0).reshape(
        own_rows, MAX_TILES, local_heads, HEAD_DIM
    )
    picked_top = jnp.take(all_top, own_places, axis=0).reshape(own_rows, MAX_TILES, local_heads)
    picked_sum = jnp.take(all_sum, own_places, axis=0).reshape(own_rows, MAX_TILES, local_heads)
    masked_top = jnp.where(live_tile[..., None], picked_top, -jnp.inf)
    peak_score = jnp.max(masked_top, axis=1)
    factor = jnp.where(live_tile[..., None], jnp.exp(picked_top - peak_score[:, None, :]), 0.0)
    numerator = jnp.sum(factor[..., None] * picked_out, axis=1)
    denominator = jnp.sum(factor * picked_sum, axis=1)
    crossed = (
        (numerator / denominator[..., None]).reshape(own_rows, head_width).astype(jnp.bfloat16)
    )
    gate_value = jnp.tanh(cross_gate[0])
    return (residual.astype(jnp.float32) + gate_value * back_project(crossed, cross_output)).astype(
        jnp.bfloat16
    )


def solution(mesh):
    in_specs = (
        P(("groups", "batch"), None),
        P(),
        P("batch", "tensor"),
        P("batch", "tensor"),
        P("tensor", "batch"),
        P(("groups", "batch"), None, "tensor"),
        P(("groups", "batch")),
        P(),
        P("batch", "tensor"),
        P(),
        P(),
        P("tensor", "batch"),
        P(),
        P(("groups", "batch"), None, "tensor"),
        P("groups"),
        P("groups", None),
    )
    out_specs = P(("groups", "batch"), None)
    return jax.shard_map(
        per_device, mesh=mesh, in_specs=in_specs, out_specs=out_specs, check_vma=False
    )
```

profile of v0, /device:TPU:0, one launch (start us, length us, event | category | flops | bytes accessed | tf_op | source)
XLA Modules:
  0.0 220.5 jit_solution(11963341826686962977)
XLA Ops:
  5.6 6.3 %all-to-all-start = ((bf16[4,2,1024]{2,1,0:T(2,128)(2,1)}), bf16[4,2,1024]{2,1,0:T(2,128)(2,1)S(1)}, u32[]{:S(2)}, u32[]{:S(2)}) async-start(bf16[4,2,1024]{2,1,0:T(2,128)(2,1)} %reshape.510), calls=%async_computation | async-start | bytes 32768 | tf_op jit(solution)/shard_map/all_to_all | solution.py:76
  13.3 3.2 %reshape.450 = bf16[4,320,2,2,128]{4,3,2,1,0:T(2,128)(2,1)S(1)} reshape(bf16[4,320,512]{2,1,0:T(8,128)(2,1)} %param.31) | data formatting | bytes 2621440 | tf_op jit(solution)/shard_map/reshape | solution.py:145
  16.4 2.9 %slice_convert_fusion = (f32[4,320,2,1,128]{4,3,2,1,0:T(1,128)S(1)}, bf16[4,320,2,1,128]{4,3,2,1,0:T(2,128)(2,1)}) fusion(bf16[4,320,2,2,128]{4,3,2,1,0:T(2,128)(2,1)S(1)} %reshape.450), kind=kLoop, calls=%fused_computation.7 | loop fusion | flops 327680 | bytes 3276800 | tf_op jit(solution)/shard_map/convert_element_type | solution.py:15
  23.6 2.3 %copy.62 = bf16[1,1024,512]{1,2,0:T(8,128)(2,1)} copy(bf16[1,1024,512]{2,1,0:T(8,128)(2,1)} %param.23) | data formatting | bytes 2097152 | tf_op args[5]
  26.9 4.6 %fusion.26 = f32[4,2048]{1,0:T(4,128)S(1)} fusion(bf16[2048,2048]{1,0:T(8,128)(2,1)} %param.20, bf16[1,4,2048]{2,0,1:T(2,128)(2,1)S(1)} %bitcast.123), kind=kOutput, calls=%fused_computation.53 | convolution fusion | flops 33554432 | bytes 8437760 | tf_op jit(solution)/shard_map/dot_general | solution.py:78
  31.5 19.9 %all-reduce = f32[4,2560]{1,0:T(4,128)S(1)} all-reduce(f32[4,2560]{1,0:T(4,128)S(1)} %pad_maximum_fusion), channel_id=2, replica_groups=mesh['groups'=2,'batch'=4,'tensor'=4] {'batch'}, use_global_device_ids=true, to_apply=%region_1.0.clone | all-reduce | flops 10240 | bytes 81920
  56.0 13.1 %all-gather = bf16[4,1,2048]{2,1,0:T(2,128)(2,1)S(1)} all-gather(bf16[1,1,2048]{2,1,0:T(2,128)(2,1)S(1)} %reshape.486), channel_id=1, replica_groups=mesh['groups'=2,'batch'=4,'tensor'=4] {'batch'}, dimensions={0}, use_global_device_ids=true | all-gather | bytes 20480 | tf_op jit(solution)/shard_map/all_gather | solution.py:39
  69.2 4.6 %convolution_bitcast_fusion.1 = f32[4,1,2048]{2,0,1:T(4,128)S(1)} fusion(bf16[2048,2048]{1,0:T(8,128)(2,1)} %param.22, bf16[4,1,2048]{2,1,0:T(2,128)(2,1)S(1)} %all-gather), kind=kOutput, calls=%fused_computation.4 | convolution fusion | flops 33554432 | bytes 8437760 | tf_op jit(solution)/shard_map/dot_general | solution.py:38
  73.8 10.3 %psum.14 = f32[4,1,2048]{2,0,1:T(4,128)S(1)} all-reduce(f32[4,1,2048]{2,0,1:T(4,128)S(1)} %convolution_bitcast_fusion.1), channel_id=1, replica_groups=mesh['groups'=2,'batch'=4,'tensor'=4] {'tensor'}, use_global_device_ids=true, to_apply=%region_4.5 | all-reduce | flops 8192 | bytes 65536 | tf_op jit(solution)/shard_map/psum | solution.py:43
  84.7 3.3 %all-to-all-start.1 = ((f32[4,1,2048]{2,1,0:T(1,128)}), f32[4,1,2048]{2,1,0:T(1,128)S(1)}, u32[]{:S(2)}, u32[]{:S(2)}) async-start(f32[4,1,2048]{2,1,0:T(1,128)} %copy.67), calls=%async_computation.1 | async-start | bytes 65536 | tf_op jit(solution)/shard_map/all_to_all | solution.py:44
  88.6 5.0 %all-to-all-done.1 = f32[4,1,2048]{2,1,0:T(1,128)S(1)} async-done(((f32[4,1,2048]{2,1,0:T(1,128)}), f32[4,1,2048]{2,1,0:T(1,128)S(1)}, u32[]{:S(2)}, u32[]{:S(2)}) %all-to-all-start.1) | async-done | bytes 32800 | tf_op jit(solution)/shard_map/all_to_all | solution.py:44
  96.3 3.3 %all-to-all-start.2 = ((bf16[4,2,1024]{2,1,0:T(2,128)(2,1)}), bf16[4,2,1024]{2,1,0:T(2,128)(2,1)S(1)}, u32[]{:S(2)}, u32[]{:S(2)}) async-start(bf16[4,2,1024]{2,1,0:T(2,128)(2,1)} %reshape.512), calls=%async_computation.2 | async-start | bytes 32768 | tf_op jit(solution)/shard_map/all_to_all | solution.py:122
  100.2 4.9 %all-to-all-done.2 = bf16[4,2,1024]{2,1,0:T(2,128)(2,1)S(1)} async-done(((bf16[4,2,1024]{2,1,0:T(2,128)(2,1)}), bf16[4,2,1024]{2,1,0:T(2,128)(2,1)S(1)}, u32[]{:S(2)}, u32[]{:S(2)}) %all-to-all-start.2) | async-done | bytes 16416 | tf_op jit(solution)/shard_map/all_to_all | solution.py:122
  105.2 4.6 %convolution_convert_fusion.1 = bf16[4,2048]{1,0:T(4,128)(2,1)S(1)} fusion(bf16[2048,2048]{1,0:T(8,128)(2,1)} %param.26, bf16[1,4,2048]{2,0,1:T(2,128)(2,1)S(1)} %bitcast.130), kind=kOutput, calls=%fused_computation.6 | convolution fusion | flops 33562624 | bytes 8421376 | tf_op jit(solution)/shard_map/dot_general | solution.py:125
  109.7 16.0 %all-reduce.1 = bf16[4,2048]{1,0:T(4,128)(2,1)S(1)} all-reduce(bf16[4,2048]{1,0:T(4,128)(2,1)S(1)} %convolution_convert_fusion.1), channel_id=3, replica_groups=mesh['groups'=2,'batch'=4,'tensor'=4] {'batch'}, use_global_device_ids=true, to_apply=%region_7.8.clone | all-reduce | flops 8192 | bytes 32768
  127.3 13.3 %all-gather.1 = bf16[4,1,2048]{2,1,0:T(2,128)(2,1)S(1)} all-gather(bf16[1,1,2048]{2,1,0:T(2,128)(2,1)S(1)} %convert_bitcast_fusion.1), channel_id=1, replica_groups=mesh['groups'=2,'batch'=4,'tensor'=4] {'batch'}, dimensions={0}, use_global_device_ids=true | all-gather | bytes 20480 | tf_op jit(solution)/shard_map/all_gather | solution.py:135
  143.0 13.4 %all-gather.3 = f32[4,4,2048]{2,1,0:T(4,128)S(1)} all-gather(f32[1,4,2048]{2,1,0:T(4,128)S(1)} %reshape.492), channel_id=1, replica_groups=mesh['groups'=2,'batch'=4,'tensor'=4] {'batch'}, dimensions={0}, use_global_device_ids=true | all-gather | bytes 163840 | tf_op jit(solution)/shard_map/all_gather | solution.py:166
  156.5 11.9 %all-gather.4 = f32[4,4,16]{2,1,0:T(4,128)S(1)} all-gather(f32[1,4,16]{2,1,0:T(4,128)S(1)} %reshape.494), channel_id=1, replica_groups=mesh['groups'=2,'batch'=4,'tensor'=4] {'batch'}, dimensions={0}, use_global_device_ids=true | all-gather | bytes 1280 | tf_op jit(solution)/shard_map/all_gather | solution.py:168
  168.3 11.9 %all-gather.2 = f32[4,4,16]{2,1,0:T(4,128)S(1)} all-gather(f32[1,4,16]{2,1,0:T(4,128)S(1)} %reshape.490), channel_id=1, replica_groups=mesh['groups'=2,'batch'=4,'tensor'=4] {'batch'}, dimensions={0}, use_global_device_ids=true | all-gather | bytes 1280 | tf_op jit(solution)/shard_map/all_gather | solution.py:167
  182.3 13.1 %all-gather.5 = bf16[4,1,2048]{2,1,0:T(2,128)(2,1)S(1)} all-gather(bf16[1,1,2048]{2,1,0:T(2,128)(2,1)S(1)} %convert_bitcast_fusion), channel_id=1, replica_groups=mesh['groups'=2,'batch'=4,'tensor'=4] {'batch'}, dimensions={0}, use_global_device_ids=true | all-gather | bytes 20480 | tf_op jit(solution)/shard_map/all_gather | solution.py:39
  195.4 4.6 %convolution_bitcast_fusion = f32[4,1,2048]{2,0,1:T(4,128)S(1)} fusion(bf16[2048,2048]{1,0:T(8,128)(2,1)} %param.29, bf16[4,1,2048]{2,1,0:T(2,128)(2,1)S(1)} %all-gather.5), kind=kOutput, calls=%fused_computation.3 | convolution fusion | flops 33554432 | bytes 8437760 | tf_op jit(solution)/shard_map/dot_general | solution.py:38
  200.0 10.3 %psum.15 = f32[4,1,2048]{2,0,1:T(4,128)S(1)} all-reduce(f32[4,1,2048]{2,0,1:T(4,128)S(1)} %convolution_bitcast_fusion), channel_id=1, replica_groups=mesh['groups'=2,'batch'=4,'tensor'=4] {'tensor'}, use_global_device_ids=true, to_apply=%region_15.17 | all-reduce | flops 8192 | bytes 65536 | tf_op jit(solution)/shard_map/psum | solution.py:43
  210.9 3.3 %all-to-all-start.3 = ((f32[4,1,2048]{2,1,0:T(1,128)}), f32[4,1,2048]{2,1,0:T(1,128)S(1)}, u32[]{:S(2)}, u32[]{:S(2)}) async-start(f32[4,1,2048]{2,1,0:T(1,128)} %copy.72), calls=%async_computation.3 | async-start | bytes 65536 | tf_op jit(solution)/shard_map/all_to_all | solution.py:44
  214.8 4.9 %all-to-all-done.3 = f32[4,1,2048]{2,1,0:T(1,128)S(1)} async-done(((f32[4,1,2048]{2,1,0:T(1,128)}), f32[4,1,2048]{2,1,0:T(1,128)S(1)}, u32[]{:S(2)}, u32[]{:S(2)}) %all-to-all-start.3) | async-done | bytes 32800 | tf_op jit(solution)/shard_map/all_to_all | solution.py:44
  (88 shorter events, 26.8 us)
Async XLA Ops:
  0.0 26.5 %copy-start = (bf16[2048,512]{1,0:T(8,128)(2,1)S(1)}, bf16[2048,512]{1,0:T(8,128)(2,1)}, u32[]{:S(2)}) copy-start(bf16[2048,512]{1,0:T(8,128)(2,1)} %param.21) | copy-start | bytes 6291460
  5.6 20.9 %all-to-all-start = ((bf16[4,2,1024]{2,1,0:T(2,128)(2,1)}), bf16[4,2,1024]{2,1,0:T(2,128)(2,1)S(1)}, u32[]{:S(2)}, u32[]{:S(2)}) async-start(bf16[4,2,1024]{2,1,0:T(2,128)(2,1)} %reshape.510), calls=%async_computation | async-start | bytes 32768 | tf_op jit(solution)/shard_map/all_to_all | solution.py:76
  19.3 1.6 copy-start.3
  19.3 2.5 %copy-start.5 = (f32[128]{0:T(128)S(1)}, f32[128]{0:T(128)}, u32[]{:S(2)}) copy-start(f32[128]{0:T(128)} %param.28) | copy-start | bytes 1540
  21.8 4.0 %copy-start.7 = (u32[32]{0:T(128)S(1)}, u32[32]{0:T(128)}, u32[]{:S(2)}) copy-start(u32[32]{0:T(128)} %constant.75) | copy-start | bytes 388
  69.2 18.8 %copy-start.2 = (bf16[8192]{0:T(1024)(128)(2,1)S(1)}, bf16[8192]{0:T(1024)(128)(2,1)}, u32[]{:S(2)}) copy-start(bf16[8192]{0:T(1024)(128)(2,1)} %param.25) | copy-start | bytes 49156
  69.2 18.8 %copy-start.6 = (s32[4]{0:T(128)S(1)}, s32[4]{0:T(128)}, u32[]{:S(2)}) copy-start(s32[4]{0:T(128)} %param.32) | copy-start | bytes 52
  69.2 24.4 %copy-start.1 = (bf16[1,8192]{1,0:T(2,128)(2,1)S(1)}, bf16[1,8192]{1,0:T(2,128)(2,1)}, u32[]{:S(2)}) copy-start(bf16[1,8192]{1,0:T(2,128)(2,1)} %param.18) | copy-start | bytes 49156
  84.7 8.9 %all-to-all-start.1 = ((f32[4,1,2048]{2,1,0:T(1,128)}), f32[4,1,2048]{2,1,0:T(1,128)S(1)}, u32[]{:S(2)}, u32[]{:S(2)}) async-start(f32[4,1,2048]{2,1,0:T(1,128)} %copy.67), calls=%async_computation.1 | async-start | bytes 65536 | tf_op jit(solution)/shard_map/all_to_all | solution.py:44
  96.3 8.8 %all-to-all-start.2 = ((bf16[4,2,1024]{2,1,0:T(2,128)(2,1)}), bf16[4,2,1024]{2,1,0:T(2,128)(2,1)S(1)}, u32[]{:S(2)}, u32[]{:S(2)}) async-start(bf16[4,2,1024]{2,1,0:T(2,128)(2,1)} %reshape.512), calls=%async_computation.2 | async-start | bytes 32768 | tf_op jit(solution)/shard_map/all_to_all | solution.py:122
  105.1 21.4 %copy-start.4 = (f32[128]{0:T(128)S(1)}, f32[128]{0:T(128)}, u32[]{:S(2)}) copy-start(f32[128]{0:T(128)} %param.27) | copy-start | bytes 1540
  210.9 8.9 %all-to-all-start.3 = ((f32[4,1,2048]{2,1,0:T(1,128)}), f32[4,1,2048]{2,1,0:T(1,128)S(1)}, u32[]{:S(2)}, u32[]{:S(2)}) async-start(f32[4,1,2048]{2,1,0:T(1,128)} %copy.72), calls=%async_computation.3 | async-start | bytes 65536 | tf_op jit(solution)/shard_map/all_to_all | solution.py:44
where the time goes:
time: 222 us; the launch traced here: 220 us
  blocking collectives  133 us (60%)
  matrix products  23.7 us (11%)
  other arithmetic  16.5 us (7%)
  starting transfers between devices  16.1 us (7%)
  waiting for transfers between devices  14.8 us (7%)
  local copies, waits for them, and re-layouts  13.2 us (6%)
  between operations  3.08 us (1%)
    unnamed x2, blocking collectives  35.9 us
    all_gather x2, blocking collectives, back_project(): lax.all_gather(values, 'batch', axis=0, tiled=True)  26.3 us
    psum x2, blocking collectives, back_project(): summed = lax.psum(partial_rows, 'tensor')  20.5 us
    all_gather x1, blocking collectives, per_device(): lax.all_gather(flat_out, 'batch', axis=0, tiled=True)  13.4 us
    all_gather x1, blocking collectives, per_device(): every_query = lax.all_gather(cross_queries, 'batch', axis=0, tiled=True)  13.3 us
    all_gather x1, blocking collectives, per_device(): lax.all_gather(flat_top, 'batch', axis=0, tiled=True)  11.9 us
    all_gather x1, blocking collectives, per_device(): lax.all_gather(flat_sum, 'batch', axis=0, tiled=True)  11.9 us
    all_to_all x2, waiting for transfers between devices, back_project(): lax.all_to_all(summed, 'batch', split_axis=0, concat_axis=1, tiled=True)  9.89 us
  transfers between devices with their start and end apart: 4, of which 3 were waited for; matrix products, arithmetic and copies ran while one was open for 7% of the time, Pallas kernels for 0%

commit v1 on v0

v1 whole, which is shorter than its diff:
```python
import functools

import jax
import jax.numpy as jnp
from jax import lax
from jax.experimental import pallas as pl
from jax.experimental.pallas import tpu as pltpu
from jax.sharding import PartitionSpec as P

HEAD_DIM = 128
MAX_TILES = 4
EPSILON = 1e-05
THETA = 500000.0
CHUNKS = 4
COLS = 256
LOW = -1e30

F32 = jnp.float32
BF16 = jnp.bfloat16


def kernel(
    dims,
    hidden,
    norms,
    tables,
    lengths,
    gate,
    counts,
    places,
    self_query,
    self_keyval,
    self_output,
    key_cache,
    cross_query,
    cross_output,
    image_keyval,
    out,
    w_sq,
    w_kv,
    w_so,
    w_cq,
    w_co,
    cache,
    image,
    keys,
    h_send,
    h_recv,
    p_send,
    p_recv,
    a_send,
    a_recv,
    s_send,
    s_recv,
    c_part,
    c_send,
    c_recv,
    o_send,
    o_recv,
    x_send,
    x_recv,
    f_send,
    f_recv,
    lhs,
    factor_rep,
    load_sem,
    send_sem,
    recv_sem,
):
    batch, tensor, width, kv_width, model, tokens = dims
    requests = batch
    depth = model // batch
    heads = width // HEAD_DIM
    kv_heads = kv_width // (2 * HEAD_DIM)
    group = heads // kv_heads
    slots = image_keyval.shape[0]
    scale = HEAD_DIM ** (-0.5)
    me = lax.axis_index("batch")
    mine = lax.axis_index("tensor")

    loads = {}

    def load(name, source, target, at, pieces=CHUNKS):
        rows = source.shape[0] // pieces
        loads[name] = [
            pltpu.make_async_copy(
                source.at[pl.ds(i * rows, rows)],
                target.at[pl.ds(i * rows, rows)],
                load_sem.at[at + i],
            )
            for i in range(pieces)
        ]

    load("sq", self_query, w_sq, 0)
    load("kv", self_keyval, w_kv, CHUNKS)
    load("so", self_output, w_so, 2 * CHUNKS)
    load("cq", cross_query, w_cq, 3 * CHUNKS)
    load("co", cross_output, w_co, 4 * CHUNKS)
    load("cache", key_cache.at[0], cache, 5 * CHUNKS)
    loads["image"] = [
        pltpu.make_async_copy(
            image_keyval.at[s], image.at[pl.ds(s * tokens, tokens)], load_sem.at[6 * CHUNKS + s]
        )
        for s in range(slots)
    ]

    def start(*names):
        for name in names:
            for copy in loads[name]:
                copy.start()

    def arrive(*names):
        for name in names:
            for copy in loads[name]:
                copy.wait()

    start("sq", "kv", "cache")

    barrier = pltpu.get_barrier_semaphore()
    for d in range(1, batch):
        pl.semaphore_signal(
            barrier,
            inc=1,
            device_id={"batch": lax.rem(me + d, batch)},
            device_id_type=pl.DeviceIdType.MESH,
        )
    for d in range(1, tensor):
        pl.semaphore_signal(
            barrier,
            inc=1,
            device_id={"tensor": lax.rem(mine + d, tensor)},
            device_id_type=pl.DeviceIdType.MESH,
        )
    for j in range(batch):
        h_send[j] = hidden[:, j * depth : (j + 1) * depth].astype(F32)
    h_recv[me] = h_send[me]
    pl.semaphore_wait(barrier, batch + tensor - 2)

    pending = []

    def exchange(phase, axis, count, index, source, target):
        copies = []
        for d in range(1, count):
            to = lax.rem(index + d, count)
            copy = pltpu.make_async_remote_copy(
                src_ref=source(to),
                dst_ref=target.at[index],
                send_sem=send_sem.at[phase, d],
                recv_sem=recv_sem.at[phase, d],
                device_id={axis: to},
                device_id_type=pl.DeviceIdType.MESH,
            )
            copy.start()
            copies.append(copy)
        pending.extend(copies)
        return copies

    def received(copies):
        for copy in copies:
            copy.wait_recv()

    def total(ref, count):
        value = ref[0]
        for j in range(1, count):
            value = value + ref[j]
        return value

    def multiply(left, weight, columns, store):
        @pl.loop(0, columns // COLS)
        def _(i):
            part = jnp.dot(
                left, weight[:, pl.ds(pl.multiple_of(i * COLS, COLS), COLS)],
                preferred_element_type=F32,
            )
            store(i, part)

    per_tile = COLS // HEAD_DIM

    copies = exchange(0, "batch", batch, me, lambda to: h_send.at[to], h_recv)
    received(copies)
    for r in range(requests):
        lhs[pl.ds(r, 1), 0:depth] = h_recv[r]
    hidden_cols = lhs[:, 0:depth]
    squares = jnp.sum(hidden_cols * hidden_cols, axis=1, keepdims=True)
    left = (hidden_cols * norms[0:1, :]).astype(BF16)

    qkv_rows = heads + 2 * kv_heads

    def store_rows(base):
        def store(i, part):
            for r in range(requests):
                for c in range(per_tile):
                    p_send[r, pl.ds(base + i * per_tile + c, 1), :] = part[
                        r : r + 1, c * HEAD_DIM : (c + 1) * HEAD_DIM
                    ]

        return store

    for r in range(requests):
        p_send[r, pl.ds(qkv_rows, 1), :] = jnp.broadcast_to(squares[r : r + 1], (1, HEAD_DIM))
    arrive("sq", "kv")
    start("so", "image", "cq", "co")
    multiply(left, w_sq, width, store_rows(0))
    multiply(left, w_kv, kv_width, store_rows(heads))
    p_recv[me] = p_send[me]
    copies = exchange(1, "batch", batch, me, lambda to: p_send.at[to], p_recv)
    arrive("cache")
    received(copies)
    projected = total(p_recv, batch)
    factor = lax.rsqrt(projected[qkv_rows : qkv_rows + 1] * (1.0 / model) + EPSILON)
    projected = projected * factor
    rotated = projected * tables[0:1, :] + pltpu.roll(projected, HEAD_DIM // 2, 1) * tables[1:2, :]

    position = lax.broadcasted_iota(jnp.int32, (group, cache.shape[0]), 1)
    usable = position < lengths[0]
    for k in range(kv_heads):
        query = rotated[k * group : (k + 1) * group].astype(BF16)
        at = heads + 2 * k
        fresh_key = rotated[at : at + 1].astype(BF16).astype(F32)
        fresh_value = projected[at + 1 : at + 2].astype(BF16).astype(F32)
        base = 2 * k * HEAD_DIM
        scores = (
            lax.dot_general(
                query,
                cache[:, base : base + HEAD_DIM],
                (((1,), (1,)), ((), ())),
                preferred_element_type=F32,
            )
            * scale
        )
        scores = jnp.where(usable, scores, LOW)
        own_score = jnp.sum(query.astype(F32) * fresh_key, axis=1, keepdims=True) * scale
        top = jnp.maximum(jnp.max(scores, axis=1, keepdims=True), own_score)
        weights = jnp.exp(scores - top)
        own_weight = jnp.exp(own_score - top)
        inverse = 1.0 / (jnp.sum(weights, axis=1, keepdims=True) + own_weight)
        mixed = jnp.dot(
            (weights * inverse).astype(BF16),
            cache[:, base + HEAD_DIM : base + 2 * HEAD_DIM],
            preferred_element_type=F32,
        )
        own_prob = (own_weight * inverse).astype(BF16).astype(F32)
        a_send[k * group : (k + 1) * group, :] = mixed + own_prob * fresh_value
    a_recv[me] = a_send[...]
    copies = exchange(2, "batch", batch, me, lambda to: a_send, a_recv)
    first = me * slots
    owners = [jnp.int32(-1)] * slots
    for r in range(requests):
        for j in range(MAX_TILES):
            at = jnp.where(j < counts[r], places[r, j] - first, -1)
            owners = [jnp.where(at == s, r, owner) for s, owner in enumerate(owners)]
    arrive("so")
    received(copies)

    for h in range(heads):
        lhs[:, h * HEAD_DIM : (h + 1) * HEAD_DIM] = a_recv[:, h, :]
    left = lhs[:, 0:width].astype(BF16)

    def store_columns(target):
        def store(i, part):
            target[:, pl.ds(pl.multiple_of(i * COLS, COLS), COLS)] = part

        return store

    multiply(left, w_so, depth, store_columns(s_send))
    s_recv[mine] = s_send[...]
    copies = exchange(3, "tensor", tensor, mine, lambda to: s_send, s_recv)

    arrive("image")
    for k in range(kv_heads):
        base = 2 * k * HEAD_DIM
        for s in range(slots):
            rows = slice(s * tokens, (s + 1) * tokens)
            raw = image[rows, base : base + HEAD_DIM].astype(F32)
            inverse = lax.rsqrt(jnp.mean(raw * raw, axis=1, keepdims=True) + EPSILON)
            keys[k, rows, :] = (raw * inverse * tables[3:4, :]).astype(BF16)
    arrive("cq")
    received(copies)
    residual = (hidden_cols + total(s_recv, tensor)).astype(BF16).astype(F32)
    squares = jnp.sum(residual * residual, axis=1, keepdims=True)
    left = (residual * norms[1:2, :]).astype(BF16)

    def store_heads(i, part):
        for c in range(per_tile):
            c_part[i * per_tile + c] = part[:, c * HEAD_DIM : (c + 1) * HEAD_DIM]

    multiply(left, w_cq, width, store_heads)
    for h in range(heads):
        c_send[h * requests : (h + 1) * requests, :] = c_part[h]
    c_send[heads * requests : (heads + 1) * requests, :] = jnp.broadcast_to(
        squares, (requests, HEAD_DIM)
    )
    c_recv[me] = c_send[...]
    copies = exchange(4, "batch", batch, me, lambda to: c_send, c_recv)
    received(copies)
    raw = total(c_recv, batch)
    factor = lax.rsqrt(
        raw[heads * requests : (heads + 1) * requests] * (1.0 / model) + EPSILON
    )
    for h in range(heads):
        factor_rep[h * requests : (h + 1) * requests, :] = factor
    raw = raw[0 : heads * requests] * factor_rep[...]
    inverse = lax.rsqrt(jnp.mean(raw * raw, axis=1, keepdims=True) + EPSILON)
    queries = (raw * inverse * tables[2:3, :]).astype(BF16)

    shape = (group * requests, slots * tokens)
    column = lax.broadcasted_iota(jnp.int32, shape, 1)
    owner = jnp.full(shape, owners[0])
    for s in range(1, slots):
        owner = jnp.where(column >= s * tokens, owners[s], owner)
    mask = lax.rem(lax.broadcasted_iota(jnp.int32, shape, 0), requests) == owner
    lane = lax.broadcasted_iota(jnp.int32, (group * requests, HEAD_DIM), 1)
    stats = jnp.zeros((group * requests, HEAD_DIM), F32)
    for k in range(kv_heads):
        base = (2 * k + 1) * HEAD_DIM
        rows = slice(k * group * requests, (k + 1) * group * requests)
        scores = (
            lax.dot_general(
                queries[rows], keys[k], (((1,), (1,)), ((), ())), preferred_element_type=F32
            )
            * scale
        )
        scores = jnp.where(mask, scores, LOW)
        top = jnp.max(scores, axis=1, keepdims=True)
        weights = jnp.where(mask, jnp.exp(scores - top), 0.0)
        amount = jnp.sum(weights, axis=1, keepdims=True)
        o_send[k] = jnp.dot(
            weights.astype(BF16), image[:, base : base + HEAD_DIM], preferred_element_type=F32
        )
        stats = jnp.where(lane == 2 * k, top, stats)
        stats = jnp.where(lane == 2 * k + 1, amount, stats)
    o_send[kv_heads] = stats
    o_recv[me] = o_send[...]
    copies = exchange(5, "batch", batch, me, lambda to: o_send, o_recv)
    arrive("co")
    received(copies)
    for k in range(kv_heads):
        tops = [o_recv[j, kv_heads, :, 2 * k : 2 * k + 1] for j in range(batch)]
        peak = functools.reduce(jnp.maximum, tops)
        factors = [jnp.exp(top - peak) for top in tops]
        amount = sum(
            f * o_recv[j, kv_heads, :, 2 * k + 1 : 2 * k + 2] for j, f in enumerate(factors)
        )
        crossed = sum(f * o_recv[j, k] for j, f in enumerate(factors)) / amount
        for g in range(group):
            h = k * group + g
            lhs[:, h * HEAD_DIM : (h + 1) * HEAD_DIM] = crossed[g * requests : (g + 1) * requests]
    left = lhs[:, 0:width].astype(BF16)

    multiply(left, w_co, depth, store_columns(x_send))
    x_recv[mine] = x_send[...]
    copies = exchange(6, "tensor", tensor, mine, lambda to: x_send, x_recv)
    amount = jnp.tanh(jnp.full((1, HEAD_DIM), gate[0]))[:, 0:1]
    received(copies)
    final = residual + amount * total(x_recv, tensor)
    for r in range(requests):
        f_send[r] = final[r : r + 1]
    f_recv[me] = f_send[me]
    copies = exchange(7, "batch", batch, me, lambda to: f_send.at[to], f_recv)
    received(copies)
    for j in range(batch):
        out[:, j * depth : (j + 1) * depth] = f_recv[j].astype(BF16)
    for copy in pending:
        copy.wait_send()


def per_device(
    hidden,
    self_norm,
    self_query,
    self_keyval,
    self_output,
    key_cache,
    cache_lengths,
    cross_norm,
    cross_query,
    query_gain,
    key_gain,
    cross_output,
    cross_gate,
    image_keyval,
    tile_count,
    tile_place,
):
    batch = lax.axis_size("batch")
    tensor = lax.axis_size("tensor")
    assert hidden.shape[0] == 1
    model = hidden.shape[1]
    depth = model // batch
    width = self_query.shape[1]
    kv_width = self_keyval.shape[1]
    heads = width // HEAD_DIM
    kv_heads = kv_width // (2 * HEAD_DIM)
    group = heads // kv_heads
    slots, tokens = image_keyval.shape[:2]
    requests = batch

    half = HEAD_DIM // 2
    frequency = THETA ** (-(jnp.arange(half, dtype=F32) * 2.0 / HEAD_DIM))
    angles = cache_lengths.astype(F32)[:, None] * frequency[None, :]
    cosine, sine = jnp.cos(angles), jnp.sin(angles)
    tables = jnp.concatenate(
        [
            jnp.concatenate([cosine, cosine], axis=1),
            jnp.concatenate([-sine, sine], axis=1),
            query_gain[None],
            key_gain[None],
        ],
        axis=0,
    )
    at = lax.axis_index("batch") * depth
    norms = jnp.stack(
        [lax.dynamic_slice(self_norm, (at,), (depth,)), lax.dynamic_slice(cross_norm, (at,), (depth,))]
    ).astype(F32)

    vmem = pl.BlockSpec(memory_space=pltpu.VMEM)
    smem = pl.BlockSpec(memory_space=pltpu.SMEM)
    anywhere = pl.BlockSpec(memory_space=pl.ANY)
    qkv_rows = -(-(heads + 2 * kv_heads + 1) // 8) * 8
    cross_rows = (heads + 1) * requests
    cross_rows = -(-cross_rows // 8) * 8
    dims = (batch, tensor, width, kv_width, model, tokens)
    return pl.pallas_call(
        functools.partial(kernel, dims),
        out_shape=jax.ShapeDtypeStruct((1, model), BF16),
        in_specs=[vmem] * 3 + [smem] * 4 + [anywhere] * 7,
        out_specs=vmem,
        scratch_shapes=[
            pltpu.VMEM(self_query.shape, BF16),
            pltpu.VMEM(self_keyval.shape, BF16),
            pltpu.VMEM(self_output.shape, BF16),
            pltpu.VMEM(cross_query.shape, BF16),
            pltpu.VMEM(cross_output.shape, BF16),
            pltpu.VMEM(key_cache.shape[1:], BF16),
            pltpu.VMEM((slots * tokens, kv_width), BF16),
            pltpu.VMEM((kv_heads, slots * tokens, HEAD_DIM), BF16),
            pltpu.VMEM((batch, 1, depth), F32),
            pltpu.VMEM((batch, 1, depth), F32),
            pltpu.VMEM((batch, qkv_rows, HEAD_DIM), F32),
            pltpu.VMEM((batch, qkv_rows, HEAD_DIM), F32),
            pltpu.VMEM((heads, HEAD_DIM), F32),
            pltpu.VMEM((batch, heads, HEAD_DIM), F32),
            pltpu.VMEM((requests, depth), F32),
            pltpu.VMEM((tensor, requests, depth), F32),
            pltpu.VMEM((heads, requests, HEAD_DIM), F32),
            pltpu.VMEM((cross_rows, HEAD_DIM), F32),
            pltpu.VMEM((batch, cross_rows, HEAD_DIM), F32),
            pltpu.VMEM((kv_heads + 1, group * requests, HEAD_DIM), F32),
            pltpu.VMEM((batch, kv_heads + 1, group * requests, HEAD_DIM), F32),
            pltpu.VMEM((requests, depth), F32),
            pltpu.VMEM((tensor, requests, depth), F32),
            pltpu.VMEM((batch, 1, depth), F32),
            pltpu.VMEM((batch, 1, depth), F32),
            pltpu.VMEM((requests, max(width, depth)), F32),
            pltpu.VMEM((heads * requests, HEAD_DIM), F32),
            pltpu.SemaphoreType.DMA((6 * CHUNKS + slots,)),
            pltpu.SemaphoreType.DMA((8, max(batch, tensor))),
            pltpu.SemaphoreType.DMA((8, max(batch, tensor))),
        ],
        compiler_params=pltpu.CompilerParams(
            collective_id=0, has_side_effects=True, vmem_limit_bytes=56 * 1024 * 1024
        ),
    )(
        hidden,
        norms,
        tables,
        cache_lengths,
        cross_gate,
        tile_count,
        tile_place,
        self_query,
        self_keyval,
        self_output,
        key_cache,
        cross_query,
        cross_output,
        image_keyval,
    )


def solution(mesh):
    in_specs = (
        P(("groups", "batch"), None),
        P(),
        P("batch", "tensor"),
        P("batch", "tensor"),
        P("tensor", "batch"),
        P(("groups", "batch"), None, "tensor"),
        P(("groups", "batch")),
        P(),
        P("batch", "tensor"),
        P(),
        P(),
        P("tensor", "batch"),
        P(),
        P(("groups", "batch"), None, "tensor"),
        P("groups"),
        P("groups", None),
    )
    out_specs = P(("groups", "batch"), None)
    return jax.shard_map(
        per_device, mesh=mesh, in_specs=in_specs, out_specs=out_specs, check_vma=False
    )
```

time: 222 us -> 55.8 us (0.25)
  blocking collectives: 133 us -> 0 us
  Pallas kernels: 0 us -> 49.3 us
  matrix products: 23.7 us -> 0 us
  starting transfers between devices: 16.1 us -> 0 us
  waiting for transfers between devices: 14.8 us -> 0 us
  other arithmetic: 16.5 us -> 2.06 us
  local copies, waits for them, and re-layouts: 13.2 us -> 2.8 us
    all_gather x6 -> x0, blocking collectives: 76.6 us -> none  [the longest x2 26.3 us: back_project(): lax.all_gather(values, 'batch', axis=0, tiled=True)]
    pallas_call x0 -> x1, Pallas kernels: none -> 49.3 us  [per_device(): pl.pallas_call(functools.partial(kernel, dims), out_shape=jax.ShapeDtypeS...]
    unnamed x2 -> x0, blocking collectives: 35.9 us -> none
    dot_general x11 -> x0, matrix products: 23.7 us -> none  [the longest x2 9.17 us: back_project(): jnp.dot(lax.all_gather(values, 'batch', axis=0, tiled=True), weight, pref...]
    psum x2 -> x0, blocking collectives: 20.5 us -> none  [back_project(): summed = lax.psum(partial_rows, 'tensor')]
    all_to_all x4 -> x0, starting transfers between devices: 16.1 us -> none  [the longest x2 6.53 us: back_project(): lax.all_to_all(summed, 'batch', split_axis=0, concat_axis=1, tiled=True)]
    all_to_all x4 -> x0, waiting for transfers between devices: 14.8 us -> none  [the longest x2 9.89 us: back_project(): lax.all_to_all(summed, 'batch', split_axis=0, concat_axis=1, tiled=True)]
    convert_element_type x6 -> x1, other arithmetic: 6.12 us -> 0.63 us  [per_device(): norms = jnp.stack([lax.dynamic_slice(self_norm, (at,), (depth,)), lax.dyn...]
  transfers between devices with their start and end apart: 4 -> 0, of which waited for: 3 -> 0; matrix products, arithmetic and copies ran while one was open for 7% -> 0% of each run, Pallas kernels for 0% -> 0%
where the time goes in v1:
time: 55.8 us; the launch traced here: 55.5 us
  Pallas kernels  49.3 us (88%)
  local copies, waits for them, and re-layouts  2.8 us (5%)
  other arithmetic  2.06 us (4%)
  between operations  1.32 us (2%)
    pallas_call x1, Pallas kernels, per_device(): pl.pallas_call(functools.partial(kernel, dims), out_shape=jax.ShapeDtypeS...  49.3 us
    unnamed x1, local copies, waits for them, and re-layouts  1.41 us
    concatenate x1, other arithmetic, per_device(): jnp.concatenate([jnp.concatenate([cosine, cosine], axis=1), jnp.concatena...  1.33 us

profile of v1, /device:TPU:0, one launch (start us, length us, event | category | flops | bytes accessed | tf_op | source)
XLA Modules:
  0.0 55.5 jit_solution(4786512077399350269)
XLA Ops:
  1.3 0.1 fusion.2
  1.4 0.1 fusion
  1.4 1.3 %pad_maximum_fusion.tables = f32[4,128]{1,0:T(4,128)} fusion(f32[1,128]{1,0:T(1,128)} %bitcast.3, f32[1,128]{1,0:T(1,128)} %bitcast.4, f32[1,64]{1,0:T(1,128)S(1)} %get-tuple-element.5, f32[1,64]{1,0:T(1,128)S(1)} %fusion.2, f32[1,64]{1,0:T(1,128)S(1)} %get-tuple-element.6), kind=kLoop, calls=%fused_computation.1 | loop fusion | flops 2560 | bytes 3840 | tf_op jit(solution)/shard_map/concatenate | solution.py:402
  2.7 0.7 %dynamic_slice.6 = bf16[2048]{0:T(1024)(128)(2,1)S(1)} dynamic-slice(bf16[8192]{0:T(1024)(128)(2,1)} %param.17, s32[]{:T(128)S(6)} %select_n.4), dynamic_slice_sizes={2048} | dynamic-slice | bytes 8196 | tf_op jit(solution)/shard_map/dynamic_slice | solution.py:413
  3.4 0.7 %dynamic_slice.7 = bf16[2048]{0:T(1024)(128)(2,1)S(1)} dynamic-slice(bf16[8192]{0:T(1024)(128)(2,1)} %param.23, s32[]{:T(128)S(6)} %select_n.4), dynamic_slice_sizes={2048} | dynamic-slice | bytes 8196 | tf_op jit(solution)/shard_map/dynamic_slice | solution.py:413
  4.1 0.6 %maximum_convert_fusion.norms = f32[2,2048]{1,0:T(2,128)} fusion(bf16[1,2048]{1,0:T(2,128)(2,1)S(1)} %stack.10, bf16[1,2048]{1,0:T(2,128)(2,1)S(1)} %stack.9), kind=kLoop, calls=%fused_computation | loop fusion | flops 16384 | bytes 24576 | tf_op jit(solution)/shard_map/convert_element_type | solution.py:414
  4.8 49.3 %shard_map.154 = bf16[1,8192]{1,0:T(2,128)(2,1)} custom-call(bf16[1,8192]{1,0:T(2,128)(2,1)} %hidden.1, f32[2,2048]{1,0:T(2,128)} %maximum_convert_fusion.norms, f32[4,128]{1,0:T(4,128)} %pad_maximum_fusion.tables, s32[1]{0:T(128)S(6)} %copy.18.lengths, f32[1]{0:T(128)S(6)} %copy.19.gate, s32[4]{0:T(128)} %counts.1, s32[4,4]{1,0:T(4,128)} %places.1, ...), custom_call_target="tpu_custom_call" | custom-call | tf_op jit(solution)/shard_map/pallas_call | solution.py:423
  54.1 1.4 %copy.20 = bf16[1,8192]{1,0:T(2,128)(2,1)} copy(bf16[1,8192]{1,0:T(2,128)(2,1)} %shard_map.154) | data formatting | bytes 32768
  (2 shorter events, 0.0 us)

commit v2 on v1

--- a/solution.py
+++ b/solution.py
@@ -22,8 +22,12 @@
 def kernel(
     dims,
     hidden,
-    norms,
-    tables,
+    self_norm,
+    cross_norm,
+    cosine,
+    sine,
+    query_gain,
+    key_gain,
     lengths,
     gate,
     counts,
@@ -50,9 +54,11 @@
     p_recv,
     a_send,
     a_recv,
+    parts,
+    stage,
     s_send,
     s_recv,
-    c_part,
+    c_stage,
     c_send,
     c_recv,
     o_send,
@@ -63,6 +69,9 @@
     f_recv,
     lhs,
     factor_rep,
+    norm_rows,
+    trig,
+    a_rows,
     load_sem,
     send_sem,
     recv_sem,
@@ -132,8 +141,16 @@
             device_id_type=pl.DeviceIdType.MESH,
         )
     for j in range(batch):
-        h_send[j] = hidden[:, j * depth : (j + 1) * depth].astype(F32)
+        columns = slice(j * depth, (j + 1) * depth)
+        h_send[j] = hidden[:, columns].astype(F32)
+        norm_rows[0, j] = self_norm[:, columns].astype(F32)
+        norm_rows[1, j] = cross_norm[:, columns].astype(F32)
     h_recv[me] = h_send[me]
+    half = HEAD_DIM // 2
+    trig[0:1, 0:half] = cosine[...]
+    trig[0:1, half:HEAD_DIM] = cosine[...]
+    trig[1:2, 0:half] = -sine[...]
+    trig[1:2, half:HEAD_DIM] = sine[...]
     pl.semaphore_wait(barrier, batch + tensor - 2)
 
     pending = []
@@ -160,10 +177,15 @@
             copy.wait_recv()
 
     def total(ref, count):
-        value = ref[0]
+        value = ref[0].astype(F32)
         for j in range(1, count):
-            value = value + ref[j]
+            value = value + ref[j].astype(F32)
         return value
+
+    def thirds(value):
+        high = value.astype(BF16).astype(F32)
+        middle = (value - high).astype(BF16).astype(F32)
+        return high, middle, value - high - middle
 
     def multiply(left, weight, columns, store):
         @pl.loop(0, columns // COLS)
@@ -182,7 +204,7 @@
         lhs[pl.ds(r, 1), 0:depth] = h_recv[r]
     hidden_cols = lhs[:, 0:depth]
     squares = jnp.sum(hidden_cols * hidden_cols, axis=1, keepdims=True)
-    left = (hidden_cols * norms[0:1, :]).astype(BF16)
+    left = (hidden_cols * norm_rows[0, me]).astype(BF16)
 
     qkv_rows = heads + 2 * kv_heads
 
@@ -209,7 +231,7 @@
     projected = total(p_recv, batch)
     factor = lax.rsqrt(projected[qkv_rows : qkv_rows + 1] * (1.0 / model) + EPSILON)
     projected = projected * factor
-    rotated = projected * tables[0:1, :] + pltpu.roll(projected, HEAD_DIM // 2, 1) * tables[1:2, :]
+    rotated = projected * trig[0:1, :] + pltpu.roll(projected, HEAD_DIM // 2, 1) * trig[1:2, :]
 
     position = lax.broadcasted_iota(jnp.int32, (group, cache.shape[0]), 1)
     usable = position < lengths[0]
@@ -240,7 +262,8 @@
             preferred_element_type=F32,
         )
         own_prob = (own_weight * inverse).astype(BF16).astype(F32)
-        a_send[k * group : (k + 1) * group, :] = mixed + own_prob * fresh_value
+        a_rows[0, k * group : (k + 1) * group, :] = mixed + own_prob * fresh_value
+    a_send[...] = a_rows[0].astype(BF16)
     a_recv[me] = a_send[...]
     copies = exchange(2, "batch", batch, me, lambda to: a_send, a_recv)
     first = me * slots
@@ -252,17 +275,31 @@
     arrive("so")
     received(copies)
 
+    for r in range(requests):
+        a_rows[r] = a_recv[r].astype(F32)
     for h in range(heads):
-        lhs[:, h * HEAD_DIM : (h + 1) * HEAD_DIM] = a_recv[:, h, :]
+        lhs[:, h * HEAD_DIM : (h + 1) * HEAD_DIM] = a_rows[:, h, :]
     left = lhs[:, 0:width].astype(BF16)
 
-    def store_columns(target):
-        def store(i, part):
-            target[:, pl.ds(pl.multiple_of(i * COLS, COLS), COLS)] = part
-
-        return store
-
-    multiply(left, w_so, depth, store_columns(s_send))
+    blocks = depth // HEAD_DIM
+
+    def store_blocks(i, part):
+        for c in range(per_tile):
+            parts[i * per_tile + c] = part[:, c * HEAD_DIM : (c + 1) * HEAD_DIM]
+
+    def pack(target):
+        for c in range(blocks):
+            stage[c * requests : (c + 1) * requests, :] = parts[c]
+        target[...] = stage[...].astype(BF16)
+
+    def unpack(ref):
+        rows = total(ref, tensor)
+        for c in range(blocks):
+            lhs[:, c * HEAD_DIM : (c + 1) * HEAD_DIM] = rows[c * requests : (c + 1) * requests]
+        return lhs[:, 0:depth]
+
+    multiply(left, w_so, depth, store_blocks)
+    pack(s_send)
     s_recv[mine] = s_send[...]
     copies = exchange(3, "tensor", tensor, mine, lambda to: s_send, s_recv)
 
@@ -273,35 +310,36 @@
             rows = slice(s * tokens, (s + 1) * tokens)
             raw = image[rows, base : base + HEAD_DIM].astype(F32)
             inverse = lax.rsqrt(jnp.mean(raw * raw, axis=1, keepdims=True) + EPSILON)
-            keys[k, rows, :] = (raw * inverse * tables[3:4, :]).astype(BF16)
+            keys[k, rows, :] = (raw * inverse * key_gain[...]).astype(BF16)
     arrive("cq")
     received(copies)
-    residual = (hidden_cols + total(s_recv, tensor)).astype(BF16).astype(F32)
+    residual = (hidden_cols + unpack(s_recv)).astype(BF16).astype(F32)
     squares = jnp.sum(residual * residual, axis=1, keepdims=True)
-    left = (residual * norms[1:2, :]).astype(BF16)
-
-    def store_heads(i, part):
-        for c in range(per_tile):
-            c_part[i * per_tile + c] = part[:, c * HEAD_DIM : (c + 1) * HEAD_DIM]
-
-    multiply(left, w_cq, width, store_heads)
+    left = (residual * norm_rows[1, me]).astype(BF16)
+
+    multiply(left, w_cq, width, store_blocks)
     for h in range(heads):
-        c_send[h * requests : (h + 1) * requests, :] = c_part[h]
-    c_send[heads * requests : (heads + 1) * requests, :] = jnp.broadcast_to(
-        squares, (requests, HEAD_DIM)
-    )
+        c_stage[h * requests : (h + 1) * requests, :] = parts[h]
+    lane = lax.broadcasted_iota(jnp.int32, (requests, HEAD_DIM), 1)
+    split = jnp.zeros((requests, HEAD_DIM), F32)
+    for i, third in enumerate(thirds(squares)):
+        split = jnp.where(lane == i, third, split)
+    rest = c_stage.shape[0] - heads * requests
+    c_stage[heads * requests :, :] = jnp.zeros((rest, HEAD_DIM), F32)
+    c_stage[heads * requests : (heads + 1) * requests, :] = split
+    c_send[...] = c_stage[...].astype(BF16)
     c_recv[me] = c_send[...]
     copies = exchange(4, "batch", batch, me, lambda to: c_send, c_recv)
     received(copies)
     raw = total(c_recv, batch)
-    factor = lax.rsqrt(
-        raw[heads * requests : (heads + 1) * requests] * (1.0 / model) + EPSILON
-    )
+    squares = jnp.sum(raw[heads * requests : (heads + 1) * requests], axis=1, keepdims=True)
+    factor = lax.rsqrt(squares * (1.0 / model) + EPSILON)
+    factor = jnp.broadcast_to(factor, (requests, HEAD_DIM))
     for h in range(heads):
         factor_rep[h * requests : (h + 1) * requests, :] = factor
     raw = raw[0 : heads * requests] * factor_rep[...]
     inverse = lax.rsqrt(jnp.mean(raw * raw, axis=1, keepdims=True) + EPSILON)
-    queries = (raw * inverse * tables[2:3, :]).astype(BF16)
+    queries = (raw * inverse * query_gain[...]).astype(BF16)
 
     shape = (group * requests, slots * tokens)
     column = lax.broadcasted_iota(jnp.int32, shape, 1)
@@ -326,40 +364,47 @@
         amount = jnp.sum(weights, axis=1, keepdims=True)
         o_send[k] = jnp.dot(
             weights.astype(BF16), image[:, base : base + HEAD_DIM], preferred_element_type=F32
-        )
-        stats = jnp.where(lane == 2 * k, top, stats)
-        stats = jnp.where(lane == 2 * k + 1, amount, stats)
-    o_send[kv_heads] = stats
+        ).astype(BF16)
+        for i, third in enumerate(thirds(top) + thirds(amount)):
+            stats = jnp.where(lane == 6 * k + i, third, stats)
+    o_send[kv_heads] = stats.astype(BF16)
     o_recv[me] = o_send[...]
     copies = exchange(5, "batch", batch, me, lambda to: o_send, o_recv)
     arrive("co")
     received(copies)
     for k in range(kv_heads):
-        tops = [o_recv[j, kv_heads, :, 2 * k : 2 * k + 1] for j in range(batch)]
+        at = 6 * k
+        blocks_in = [o_recv[j, kv_heads].astype(F32) for j in range(batch)]
+        tops, sums = [
+            [
+                b[:, i : i + 1] + b[:, i + 1 : i + 2] + b[:, i + 2 : i + 3]
+                for b in blocks_in
+            ]
+            for i in (at, at + 3)
+        ]
         peak = functools.reduce(jnp.maximum, tops)
         factors = [jnp.exp(top - peak) for top in tops]
-        amount = sum(
-            f * o_recv[j, kv_heads, :, 2 * k + 1 : 2 * k + 2] for j, f in enumerate(factors)
-        )
-        crossed = sum(f * o_recv[j, k] for j, f in enumerate(factors)) / amount
+        amount = sum(f * part for f, part in zip(factors, sums))
+        crossed = sum(f * o_recv[j, k].astype(F32) for j, f in enumerate(factors)) / amount
         for g in range(group):
             h = k * group + g
             lhs[:, h * HEAD_DIM : (h + 1) * HEAD_DIM] = crossed[g * requests : (g + 1) * requests]
     left = lhs[:, 0:width].astype(BF16)
 
-    multiply(left, w_co, depth, store_columns(x_send))
+    multiply(left, w_co, depth, store_blocks)
+    pack(x_send)
     x_recv[mine] = x_send[...]
     copies = exchange(6, "tensor", tensor, mine, lambda to: x_send, x_recv)
-    amount = jnp.tanh(jnp.full((1, HEAD_DIM), gate[0]))[:, 0:1]
-    received(copies)
-    final = residual + amount * total(x_recv, tensor)
+    gating = jnp.tanh(jnp.full((1, HEAD_DIM), gate[0]))[:, 0:1]
+    received(copies)
+    final = residual + gating * unpack(x_recv)
     for r in range(requests):
         f_send[r] = final[r : r + 1]
     f_recv[me] = f_send[me]
     copies = exchange(7, "batch", batch, me, lambda to: f_send.at[to], f_recv)
     received(copies)
     for j in range(batch):
-        out[:, j * depth : (j + 1) * depth] = f_recv[j].astype(BF16)
+        out[:, j * depth : (j + 1) * depth] = f_recv[j]
     for copy in pending:
         copy.wait_send()
 
@@ -399,31 +444,19 @@
     frequency = THETA ** (-(jnp.arange(half, dtype=F32) * 2.0 / HEAD_DIM))
     angles = cache_lengths.astype(F32)[:, None] * frequency[None, :]
     cosine, sine = jnp.cos(angles), jnp.sin(angles)
-    tables = jnp.concatenate(
-        [
-            jnp.concatenate([cosine, cosine], axis=1),
-            jnp.concatenate([-sine, sine], axis=1),
-            query_gain[None],
-            key_gain[None],
-        ],
-        axis=0,
-    )
-    at = lax.axis_index("batch") * depth
-    norms = jnp.stack(
-        [lax.dynamic_slice(self_norm, (at,), (depth,)), lax.dynamic_slice(cross_norm, (at,), (depth,))]
-    ).astype(F32)
-
     vmem = pl.BlockSpec(memory_space=pltpu.VMEM)
     smem = pl.BlockSpec(memory_space=pltpu.SMEM)
     anywhere = pl.BlockSpec(memory_space=pl.ANY)
     qkv_rows = -(-(heads + 2 * kv_heads + 1) // 8) * 8
-    cross_rows = (heads + 1) * requests
-    cross_rows = -(-cross_rows // 8) * 8
+    cross_rows = -(-(heads + 1) * requests // 16) * 16
+    head_rows = -(-heads // 16) * 16
+    blocks = depth // HEAD_DIM
+    sum_rows = blocks * requests
     dims = (batch, tensor, width, kv_width, model, tokens)
-    return pl.pallas_call(
+    result = pl.pallas_call(
         functools.partial(kernel, dims),
-        out_shape=jax.ShapeDtypeStruct((1, model), BF16),
-        in_specs=[vmem] * 3 + [smem] * 4 + [anywhere] * 7,
+        out_shape=jax.ShapeDtypeStruct((1, model), F32),
+        in_specs=[vmem] * 7 + [smem] * 4 + [anywhere] * 7,
         out_specs=vmem,
         scratch_shapes=[
             pltpu.VMEM(self_query.shape, BF16),
@@ -438,21 +471,26 @@
             pltpu.VMEM((batch, 1, depth), F32),
             pltpu.VMEM((batch, qkv_rows, HEAD_DIM), F32),
             pltpu.VMEM((batch, qkv_rows, HEAD_DIM), F32),
-            pltpu.VMEM((heads, HEAD_DIM), F32),
-            pltpu.VMEM((batch, heads, HEAD_DIM), F32),
-            pltpu.VMEM((requests, depth), F32),
-            pltpu.VMEM((tensor, requests, depth), F32),
-            pltpu.VMEM((heads, requests, HEAD_DIM), F32),
+            pltpu.VMEM((head_rows, HEAD_DIM), BF16),
+            pltpu.VMEM((batch, head_rows, HEAD_DIM), BF16),
+            pltpu.VMEM((max(heads, blocks), requests, HEAD_DIM), F32),
+            pltpu.VMEM((sum_rows, HEAD_DIM), F32),
+            pltpu.VMEM((sum_rows, HEAD_DIM), BF16),
+            pltpu.VMEM((tensor, sum_rows, HEAD_DIM), BF16),
             pltpu.VMEM((cross_rows, HEAD_DIM), F32),
-            pltpu.VMEM((batch, cross_rows, HEAD_DIM), F32),
-            pltpu.VMEM((kv_heads + 1, group * requests, HEAD_DIM), F32),
-            pltpu.VMEM((batch, kv_heads + 1, group * requests, HEAD_DIM), F32),
-            pltpu.VMEM((requests, depth), F32),
-            pltpu.VMEM((tensor, requests, depth), F32),
+            pltpu.VMEM((cross_rows, HEAD_DIM), BF16),
+            pltpu.VMEM((batch, cross_rows, HEAD_DIM), BF16),
+            pltpu.VMEM((kv_heads + 1, group * requests, HEAD_DIM), BF16),
+            pltpu.VMEM((batch, kv_heads + 1, group * requests, HEAD_DIM), BF16),
+            pltpu.VMEM((sum_rows, HEAD_DIM), BF16),
+            pltpu.VMEM((tensor, sum_rows, HEAD_DIM), BF16),
             pltpu.VMEM((batch, 1, depth), F32),
             pltpu.VMEM((batch, 1, depth), F32),
             pltpu.VMEM((requests, max(width, depth)), F32),
             pltpu.VMEM((heads * requests, HEAD_DIM), F32),
+            pltpu.VMEM((2, batch, 1, depth), F32),
+            pltpu.VMEM((8, HEAD_DIM), F32),
+            pltpu.VMEM((batch, head_rows, HEAD_DIM), F32),
             pltpu.SemaphoreType.DMA((6 * CHUNKS + slots,)),
             pltpu.SemaphoreType.DMA((8, max(batch, tensor))),
             pltpu.SemaphoreType.DMA((8, max(batch, tensor))),
@@ -462,8 +500,12 @@
         ),
     )(
         hidden,
-        norms,
-        tables,
+        self_norm[None],
+        cross_norm[None],
+        cosine,
+        sine,
+        query_gain[None],
+        key_gain[None],
         cache_lengths,
         cross_gate,
         tile_count,
@@ -476,6 +518,7 @@
         cross_output,
         image_keyval,
     )
+    return result.astype(BF16)
 
 
 def solution(mesh):

time: 55.8 us -> 52.9 us (0.948)
  Pallas kernels: 49.3 us -> 46.5 us
    pallas_call x1, Pallas kernels: 49.3 us -> 46.5 us  [per_device(): pl.pallas_call(functools.partial(kernel, dims), out_shape=jax.ShapeDtypeS...]
    broadcast_in_dim x0 -> x2, local copies, waits for them, and re-layouts: none -> 2.7 us  [the longest x1 1.35 us: per_device(): cross_norm[None]]
    unnamed x1 -> x0, local copies, waits for them, and re-layouts: 1.41 us -> none
    dynamic_slice x2 -> x0, local copies, waits for them, and re-layouts: 1.37 us -> none  [the longest x1 0.69 us: per_device(): lax.dynamic_slice(self_norm, (at,), (depth,))]
    concatenate x1 -> x0, other arithmetic: 1.33 us -> none  [per_device(): jnp.concatenate([jnp.concatenate([cosine, cosine], axis=1), jnp.concatena...]
    convert_element_type x1, other arithmetic: 0.63 us -> 1.4 us  [per_device(): return result.astype(BF16)]
where the time goes in v2:
time: 52.9 us; the launch traced here: 52.5 us
  Pallas kernels  46.5 us (88%)
  local copies, waits for them, and re-layouts  2.7 us (5%)
  other arithmetic  1.98 us (4%)
  between operations  1.31 us (2%)
    pallas_call x1, Pallas kernels, per_device(): pl.pallas_call(functools.partial(kernel, dims), out_shape=jax.ShapeDtypeS...  46.5 us
    convert_element_type x1, other arithmetic, per_device(): return result.astype(BF16)  1.4 us
    broadcast_in_dim x1, local copies, waits for them, and re-layouts, per_device(): cross_norm[None]  1.35 us
    broadcast_in_dim x1, local copies, waits for them, and re-layouts, per_device(): self_norm[None]  1.35 us

profile of v2, /device:TPU:0, one launch (start us, length us, event | category | flops | bytes accessed | tf_op | source)
XLA Modules:
  0.0 52.5 jit_solution(7266914998555749670)
XLA Ops:
  1.3 0.6 %fusion = (f32[1,64]{1,0:T(1,128)}, f32[1,64]{1,0:T(1,128)}) fusion(f32[]{:T(128)} %bitcast), kind=kLoop, calls=%fused_computation.1 | loop fusion | flops 192 | bytes 516 | tf_op jit(solution)/shard_map/sin | solution.py:446
  1.9 1.4 %broadcast_in_dim.14.self_norm = bf16[1,8192]{1,0:T(2,128)(2,1)} reshape(bf16[8192]{0:T(1024)(128)(2,1)} %param.17) | data formatting | bytes 32768 | tf_op jit(solution)/shard_map/broadcast_in_dim | solution.py:503
  3.2 1.4 %broadcast_in_dim.15.cross_norm = bf16[1,8192]{1,0:T(2,128)(2,1)} reshape(bf16[8192]{0:T(1024)(128)(2,1)} %param.23) | data formatting | bytes 32768 | tf_op jit(solution)/shard_map/broadcast_in_dim | solution.py:504
  4.6 46.5 %shard_map.154 = f32[1,8192]{1,0:T(1,128)} custom-call(bf16[1,8192]{1,0:T(2,128)(2,1)} %hidden.1, bf16[1,8192]{1,0:T(2,128)(2,1)} %broadcast_in_dim.14.self_norm, bf16[1,8192]{1,0:T(2,128)(2,1)} %broadcast_in_dim.15.cross_norm, f32[1,64]{1,0:T(1,128)} %get-tuple-element.6.cosine, f32[1,64]{1,0:T(1,128)} %get-tuple-element.5.sine, f32[1,128]{1,0:T(1,128)} %bitcast.3, ...), custom_call_target="tpu_custom_call" | custom-call | tf_op jit(solution)/shard_map/pallas_call | solution.py:456
  51.1 1.4 %convert_element_type.7 = bf16[1,8192]{1,0:T(2,128)(2,1)} convert(f32[1,8192]{1,0:T(1,128)} %shard_map.154) | non-fusion elementwise | flops 8192 | bytes 49152 | tf_op jit(solution)/shard_map/convert_element_type | solution.py:521

commit v3 on v2

--- a/solution.py
+++ b/solution.py
@@ -143,8 +143,8 @@
     for j in range(batch):
         columns = slice(j * depth, (j + 1) * depth)
         h_send[j] = hidden[:, columns].astype(F32)
-        norm_rows[0, j] = self_norm[:, columns].astype(F32)
-        norm_rows[1, j] = cross_norm[:, columns].astype(F32)
+        norm_rows[0, j] = self_norm[columns].astype(F32).reshape(1, depth)
+        norm_rows[1, j] = cross_norm[columns].astype(F32).reshape(1, depth)
     h_recv[me] = h_send[me]
     half = HEAD_DIM // 2
     trig[0:1, 0:half] = cosine[...]
@@ -500,8 +500,8 @@
         ),
     )(
         hidden,
-        self_norm[None],
-        cross_norm[None],
+        self_norm,
+        cross_norm,
         cosine,
         sine,
         query_gain[None],

time: 52.9 us -> 50.1 us (0.947)
  local copies, waits for them, and re-layouts: 2.7 us -> 0 us
    broadcast_in_dim x2 -> x0, local copies, waits for them, and re-layouts: 2.7 us -> none  [the longest x1 1.35 us: per_device(): cross_norm[None]]
where the time goes in v3:
time: 50.1 us; the launch traced here: 49.9 us
  Pallas kernels  46.5 us (93%)
  other arithmetic  2.03 us (4%)
  between operations  1.31 us (3%)
    pallas_call x1, Pallas kernels, per_device(): pl.pallas_call(functools.partial(kernel, dims), out_shape=jax.ShapeDtypeS...  46.5 us
    convert_element_type x1, other arithmetic, per_device(): return result.astype(BF16)  1.4 us

profile of v3, /device:TPU:0, one launch (start us, length us, event | category | flops | bytes accessed | tf_op | source)
XLA Modules:
  0.0 49.9 jit_solution(4030089371777667799)
XLA Ops:
  1.3 0.6 %fusion = (f32[1,64]{1,0:T(1,128)}, f32[1,64]{1,0:T(1,128)}) fusion(f32[]{:T(128)} %bitcast), kind=kLoop, calls=%fused_computation.1 | loop fusion | flops 192 | bytes 516 | tf_op jit(solution)/shard_map/sin | solution.py:446
  1.9 46.5 %shard_map.154 = f32[1,8192]{1,0:T(1,128)} custom-call(bf16[1,8192]{1,0:T(2,128)(2,1)} %hidden.1, bf16[8192]{0:T(1024)(128)(2,1)} %self_norm.1, bf16[8192]{0:T(1024)(128)(2,1)} %cross_norm.1, f32[1,64]{1,0:T(1,128)} %get-tuple-element.6.cosine, f32[1,64]{1,0:T(1,128)} %get-tuple-element.5.sine, f32[1,128]{1,0:T(1,128)} %bitcast.3, f32[1,128]{1,0:T(1,128)} %bitcast.4, ...), custom_call_target="tpu_custom_call" | custom-call | tf_op jit(solution)/shard_map/pallas_call | solution.py:456
  48.5 1.4 %convert_element_type.7 = bf16[1,8192]{1,0:T(2,128)(2,1)} convert(f32[1,8192]{1,0:T(1,128)} %shard_map.154) | non-fusion elementwise | flops 8192 | bytes 49152 | tf_op jit(solution)/shard_map/convert_element_type | solution.py:521
